TPU v7x, 256 devices: a whole 4x4x8 slice. The times are simulated.
256 devices in a mesh: sfc: 64 (over z, y, core), lev: 4 (over x).
Axes of the slice: x: 4, y: 4, z: 8, core: 2. Of those that a mesh axis runs over, the one named last changes fastest.
Arguments:
- tracers: float32 [16, 40, 32768], P('lev', None, 'sfc'), may hold values from 0.1 to 4
- owners: int32 [2, 16, 32768], P(None, 'lev', 'sfc'), may hold values from 0 to 63, as said below
- source_elements: int32 [2, 16, 32768], P(None, 'lev', 'sfc'), may hold values from 0 to 31, as said below
- ref_coords: float32 [2, 2, 16, 32768], P(None, None, 'lev', 'sfc'), may hold values from -1 to 1
- node_mass: float32 [32768], P('sfc'), may hold values from 0.4 to 2.5
- neighbours: int32 [3, 32768], P(None, 'sfc'), may hold values from -1 to 32767, as said below
- lift_fraction: float32 [16, 32768], P('lev', 'sfc'), may hold values from 0 to 0.8
Outputs:
- transported: float32 [16, 40, 32768], P('lev', None, 'sfc')
Inputs may be any that keep to these rules, and one draw needn't show every extreme that they name: Elements form a torus of 256 rows by 8 columns numbered row by row; block b holds rows 4 b to 4 b + 3. The source element named by owners and source_elements is the node's own element or one of its eight neighbours on this torus, so the owner is the node's block, the previous or the next one (the last block's next is the first). In every substep and level, at most 128 nodes of one block name the previous block and at most 128 the next; each bound is reached by some block. `source_elements`: drawn together with owners, as described there. Each entry is -1 or the index of another copy of the same grid point; copies name each other; a node has 0, 1 or 3 other copies. The element of a copy is one of the eight neighbours of the node's element on the torus described for owners.
All inputs are finite; a program needn't handle non-finite values.
Results may differ from a plain program's by a relative error of at most 0.0001.
Values sent between devices are 32-bit elements; how exact they have to be, the bound alone decides.
A program may use at most 128 MiB of HBM per device.

v0:
```python
import functools

import jax
import jax.numpy as jnp
from jax import lax
from jax.experimental import pallas as pl
from jax.experimental.pallas import tpu as pltpu
from jax.sharding import PartitionSpec as P

GLL_POINTS = (-1.0, -0.4472135954999579, 0.4472135954999579, 1.0)
MESH = pl.DeviceIdType.MESH
BF16 = jnp.bfloat16
F32 = jnp.float32
LEVELS = 4
TRACERS = 40
ROW = 128
BLOCK = 512


def basis_tables():
    node = lax.broadcasted_iota(jnp.int32, (16, ROW), 0)

    def pick(index, values):
        out = jnp.full((16, ROW), values[3], F32)
        for k in range(3):
            out = jnp.where(index == k, values[k], out)
        return out

    others = [[x for k, x in enumerate(GLL_POINTS) if k != i] for i in range(4)]
    scale = []
    for i in range(4):
        product = 1.0
        for x in others[i]:
            product *= GLL_POINTS[i] - x
        scale.append(1.0 / product)
    first, second = node >> 2, node & 3
    points_a = [pick(first, [others[i][k] for i in range(4)]) for k in range(3)]
    points_b = [pick(second, [others[i][k] for i in range(4)]) for k in range(3)]
    return points_a, points_b, pick(first, scale) * pick(second, scale)


def split(values):
    high = values.astype(BF16).astype(F32)
    return jnp.concatenate([high, values - high], axis=0).astype(BF16)


def spread(row):
    return jnp.broadcast_to(row, (16, ROW))


def kernel(
    tracers, owners, elements, coords, mass, neighbours, lift,
    out,
    field_prev, field_own, field_next, own_ids, elem_ids, refs, masses, copies, lifts, prepared,
    weights1, weights2, shared, inverse, stage0, stage1, stage2, stage3, result, above,
    local_sem, send_dep, recv_dep, send_field, recv_field, send_up, recv_up,
):
    me = lax.axis_index("sfc")
    peers = lax.axis_size("sfc")
    group = lax.axis_index("lev")
    groups = lax.axis_size("lev")
    after = lax.rem(me + 1, peers)
    before = lax.rem(me + peers - 1, peers)

    barrier = pltpu.get_barrier_semaphore()
    for device in (before, after):
        pl.semaphore_signal(barrier, inc=1, device_id={"sfc": device}, device_id_type=MESH)

    @pl.when(group < groups - 1)
    def _():
        pl.semaphore_signal(barrier, inc=1, device_id={"lev": group + 1}, device_id_type=MESH)

    local = []

    def fetch(source, target):
        copy = pltpu.make_async_copy(source, target, local_sem.at[len(local)])
        copy.start()
        local.append(copy)

    fetch(owners, own_ids.at[1])
    fetch(elements, elem_ids.at[1])
    fetch(coords, refs.at[1])
    fetch(mass, masses.at[1])
    fetch(neighbours, copies.at[1])
    fetch(lift, lifts)
    fetch(tracers, field_own)

    pl.semaphore_wait(barrier, jnp.where(group > 0, 3, 2))

    sides = ((after, 0, BLOCK - ROW, field_prev), (before, 2, 0, field_next))
    deps = []
    for side, (device, slot, edge, _) in enumerate(sides):
        pieces = (
            (owners.at[0], own_ids.at[slot, 0]),
            (elements.at[0], elem_ids.at[slot, 0]),
            (coords.at[0], refs.at[slot, 0]),
            (mass, masses.at[slot]),
            (neighbours, copies.at[slot]),
            (owners.at[1, :, pl.ds(edge, ROW)], own_ids.at[slot, 1, :, pl.ds(edge, ROW)]),
            (elements.at[1, :, pl.ds(edge, ROW)], elem_ids.at[slot, 1, :, pl.ds(edge, ROW)]),
            (coords.at[1, :, :, pl.ds(edge, ROW)], refs.at[slot, 1, :, :, pl.ds(edge, ROW)]),
        )
        deps.append(
            [
                pltpu.make_async_remote_copy(
                    src_ref=source,
                    dst_ref=target,
                    send_sem=send_dep.at[side, number],
                    recv_sem=recv_dep.at[side, number],
                    device_id={"sfc": device},
                    device_id_type=MESH,
                )
                for number, (source, target) in enumerate(pieces)
            ]
        )
    for pair in zip(*deps):
        for copy in pair:
            copy.start()

    def field_copy(side, level):
        device, _, _, target = sides[side]
        return pltpu.make_async_remote_copy(
            src_ref=tracers.at[level],
            dst_ref=target.at[level],
            send_sem=send_field.at[side, level],
            recv_sem=recv_field.at[side, level],
            device_id={"sfc": device},
            device_id_type=MESH,
        )

    for level in range(LEVELS):
        for side in range(2):
            field_copy(side, level).start()

    points_a, points_b, scale = basis_tables()
    row_mask = 4 * peers - 1
    point_mask = BLOCK * peers - 1
    node = lax.broadcasted_iota(jnp.int32, (16, ROW), 0)
    lane = lax.broadcasted_iota(jnp.int32, (16, ROW), 1)
    zero = jnp.zeros((16, ROW), BF16)
    own_elem = (8 + (lane >> 4)).astype(F32).astype(BF16)
    own_pick = jnp.where((lane & 15) == node, 1.0, 0.0).astype(BF16)

    def prepare(slot, step, rows):
        lanes = pl.ds(rows[0] * ROW, len(rows) * ROW)
        width = len(rows) * ROW
        row = lax.broadcasted_iota(jnp.int32, (LEVELS, width), 1) // ROW + rows[0]
        elem = elem_ids[slot, step, :, lanes]
        source_row = own_ids[slot, step, :, lanes] * 4 + (elem >> 3)
        above_row = (me + (slot - 1)) * 4 - 1 + row
        offset = (source_row - above_row) & row_mask
        code = (offset * 8 + (elem & 7)).astype(F32)
        for level in range(LEVELS):
            prepared[slot, step, level, 0:1, lanes] = code[level : level + 1]
            prepared[slot, step, level, 1:2, lanes] = refs[slot, step, 0, level : level + 1, lanes]
            prepared[slot, step, level, 2:3, lanes] = refs[slot, step, 1, level : level + 1, lanes]

    def build_weights(slot, row, step, level, target, pair, place):
        lanes = pl.ds(row * ROW, ROW)
        code = spread(prepared[slot, step, level, 0:1, lanes]).astype(BF16)
        a = spread(prepared[slot, step, level, 1:2, lanes])
        b = spread(prepared[slot, step, level, 2:3, lanes])
        weight = spread(masses[slot, :, lanes]) * scale
        for point in points_a:
            weight = weight * (a - point)
        for point in points_b:
            weight = weight * (b - point)
        high = weight.astype(BF16)
        low = (weight - high.astype(F32)).astype(BF16)
        start = ROW * place
        for number in range(24):
            hit = code == jnp.asarray(number, BF16)
            rows = pl.ds(start + 16 * number, 16)
            target[level, pair, rows, pl.ds(start, ROW)] = jnp.where(hit, high, zero)
            target[level, pair, rows, pl.ds(256 + start, ROW)] = jnp.where(hit, low, zero)
        blank = jnp.zeros((ROW, ROW), BF16)
        rows = pl.ds(0 if place else 384, ROW)
        target[level, pair, rows, pl.ds(start, ROW)] = blank
        target[level, pair, rows, pl.ds(256 + start, ROW)] = blank

    def build_shared(slot, row, pair, place):
        lanes = pl.ds(row * ROW, ROW)
        first = ((me + (slot - 1)) * 4 + (row - 1)) * ROW
        codes, picks = [], []
        for number in range(3):
            copy = copies[slot, pl.ds(number, 1), lanes]
            offset = (copy - first) & point_mask
            code = jnp.where(copy >= 0, offset >> 4, -1)
            codes.append(spread(code.astype(F32)).astype(BF16))
            picks.append(jnp.where(spread(offset & 15) == node, 1.0, 0.0).astype(BF16))
        start = ROW * place
        for number in range(24):
            count = jnp.asarray(number, BF16)
            value = zero
            for code, pick in zip(codes, picks):
                value = value + jnp.where(code == count, pick, zero)
            if 8 <= number < 16:
                value = value + jnp.where(own_elem == count, own_pick, zero)
            shared[pair, pl.ds(start + 16 * number, 16), pl.ds(start, ROW)] = value
        rows = pl.ds(0 if place else 384, ROW)
        shared[pair, rows, pl.ds(start, ROW)] = jnp.zeros((ROW, ROW), BF16)

    def moved1_row(extended, level):
        build_weights(extended // 4, extended % 4, 0, level, weights1, (extended - 1) // 2, (extended - 1) % 2)

    def moved2_row(extended, level):
        build_weights(extended // 4, extended % 4, 1, level, weights2, (extended - 3) // 2, (extended - 3) % 2)

    def shared_row(extended):
        build_shared(extended // 4, extended % 4, (extended - 2) // 2, (extended - 2) % 2)

    for copy in local:
        copy.wait()

    for step in range(2):
        prepare(1, step, (0, 1, 2, 3))

    def own_level(level, carry):
        for extended in range(4, 8):
            moved1_row(extended, level)
            moved2_row(extended, level)
        return carry

    lax.fori_loop(0, LEVELS, own_level, 0)
    for extended in range(4, 8):
        shared_row(extended)

    for side in range(2):
        for copy in deps[side]:
            copy.wait_recv()
    prepare(0, 0, (1, 2, 3))
    prepare(2, 0, (0, 1, 2))
    prepare(0, 1, (3,))
    prepare(2, 1, (0,))
    for extended in (2, 3, 8, 9):
        shared_row(extended)

    piece = lax.broadcasted_iota(jnp.int32, (16, BLOCK), 0)
    parts = []
    for slot in range(3):
        whole = masses[slot]
        high = whole.astype(BF16).astype(F32)
        middle = (whole - high).astype(BF16).astype(F32)
        low = whole - high - middle
        mixed = jnp.where(piece == 0, high, jnp.where(piece == 1, middle, jnp.where(piece == 2, low, 0.0)))
        parts.append(mixed.astype(BF16))
    mass_rows = jnp.concatenate(parts, axis=1)
    for pair in range(4):
        begin = ROW + 256 * pair
        total = jnp.dot(mass_rows[:, begin : begin + 512], shared[pair], preferred_element_type=F32)
        inverse[pair] = 1.0 / jnp.sum(total, axis=0, keepdims=True)

    def interpolate(values, table):
        product = jnp.dot(values, table, preferred_element_type=F32)
        low = product[:TRACERS, 256:] + product[TRACERS:, :256] + product[TRACERS:, 256:]
        return product[:TRACERS, :256] + low

    def average(values, pair):
        product = jnp.dot(values, shared[pair], preferred_element_type=F32)
        return (product[:TRACERS] + product[TRACERS:]) * inverse[pair]

    def up_copy():
        return pltpu.make_async_remote_copy(
            src_ref=result.at[0],
            dst_ref=above,
            send_sem=send_up,
            recv_sem=recv_up,
            device_id={"lev": group - 1},
            device_id_type=MESH,
        )

    def one_level(level, carry):
        for extended in (1, 2, 3, 8, 9, 10):
            moved1_row(extended, level)
        for extended in (3, 8):
            moved2_row(extended, level)
        stage0[:, 512:1024] = split(field_own[level])
        for side in range(2):
            field_copy(side, level).wait_recv()
        stage0[:, :512] = split(field_prev[level])
        stage0[:, 1024:] = split(field_next[level])
        for pair in range(5):
            at = 256 * pair
            stage1[:, at : at + 256] = split(interpolate(stage0[:, at : at + 512], weights1[level, pair]))
        for pair in range(4):
            at = 256 * pair
            stage2[:, at : at + 256] = split(average(stage1[:, at : at + 512], pair))
        for pair in range(3):
            at = 256 * pair
            stage3[:, at : at + 256] = split(interpolate(stage2[:, at : at + 512], weights2[level, pair]))
        for pair in range(2):
            at = 256 * pair
            result[level, :, at : at + 256] = average(stage3[:, at : at + 512], pair + 1)

        @pl.when((level == 0) & (group > 0))
        def _():
            up_copy().start()

        return carry

    lax.fori_loop(0, LEVELS, one_level, 0)

    for level in range(LEVELS - 1):
        field = result[level]
        out[level] = field + lifts[pl.ds(level, 1), :] * (result[level + 1] - field)

    for side in range(2):
        for copy in deps[side]:
            copy.wait_send()
        for level in range(LEVELS):
            field_copy(side, level).wait_send()

    last = LEVELS - 1

    @pl.when(group > 0)
    def _():
        up_copy().wait_send()

    @pl.when(group < groups - 1)
    def _():
        up_copy().wait_recv()
        field = result[last]
        out[last] = field + lifts[pl.ds(last, 1), :] * (above[...] - field)

    @pl.when(group == groups - 1)
    def _():
        field = result[last]
        out[last] = field + lifts[pl.ds(last, 1), :] * (field - field)


def local(tracers, owners, source_elements, ref_coords, node_mass, neighbours, lift_fraction):
    dma = pltpu.SemaphoreType.DMA
    return pl.pallas_call(
        kernel,
        out_shape=jax.ShapeDtypeStruct(tracers.shape, F32),
        in_specs=[pl.BlockSpec(memory_space=pltpu.HBM)] * 7,
        out_specs=pl.BlockSpec(memory_space=pltpu.VMEM),
        scratch_shapes=[
            pltpu.VMEM((LEVELS, TRACERS, BLOCK), F32),
            pltpu.VMEM((LEVELS, TRACERS, BLOCK), F32),
            pltpu.VMEM((LEVELS, TRACERS, BLOCK), F32),
            pltpu.VMEM((3, 2, LEVELS, BLOCK), jnp.int32),
            pltpu.VMEM((3, 2, LEVELS, BLOCK), jnp.int32),
            pltpu.VMEM((3, 2, 2, LEVELS, BLOCK), F32),
            pltpu.VMEM((3, 1, BLOCK), F32),
            pltpu.VMEM((3, 3, BLOCK), jnp.int32),
            pltpu.VMEM((LEVELS, BLOCK), F32),
            pltpu.VMEM((3, 2, LEVELS, 3, BLOCK), F32),
            pltpu.VMEM((LEVELS, 5, 512, 512), BF16),
            pltpu.VMEM((LEVELS, 3, 512, 512), BF16),
            pltpu.VMEM((4, 512, 256), BF16),
            pltpu.VMEM((4, 1, 256), F32),
            pltpu.VMEM((2 * TRACERS, 1536), BF16),
            pltpu.VMEM((2 * TRACERS, 1280), BF16),
            pltpu.VMEM((2 * TRACERS, 1024), BF16),
            pltpu.VMEM((2 * TRACERS, 768), BF16),
            pltpu.VMEM((LEVELS, TRACERS, BLOCK), F32),
            pltpu.VMEM((TRACERS, BLOCK), F32),
            dma((7,)),
            dma((2, 8)),
            dma((2, 8)),
            dma((2, LEVELS)),
            dma((2, LEVELS)),
            dma,
            dma,
        ],
        compiler_params=pltpu.CompilerParams(
            collective_id=0, has_side_effects=True, vmem_limit_bytes=32 << 20
        ),
    )(*(pltpu.with_memory_space_constraint(x, pltpu.HBM) for x in (tracers, owners, source_elements, ref_coords, node_mass.reshape(1, -1), neighbours, lift_fraction)))


def solution(mesh):
    in_specs = (
        P("lev", None, "sfc"),
        P(None, "lev", "sfc"),
        P(None, "lev", "sfc"),
        P(None, None, "lev", "sfc"),
        P("sfc"),
        P(None, "sfc"),
        P("lev", "sfc"),
    )
    out_specs = P("lev", None, "sfc")
    return jax.shard_map(local, mesh=mesh, in_specs=in_specs, out_specs=out_specs, check_vma=False)
```

profile of v0, /device:TPU:2, one launch (start us, length us, event | category | flops | bytes accessed | tf_op | source)
XLA Modules:
  0.0 18.3 jit_solution(4181852017483576556)
XLA Ops:
  0.0 17.6 %shard_map.73 = f32[4,40,512]{2,1,0:T(8,128)S(1)} custom-call(f32[4,40,512]{2,1,0:T(8,128)} %tracers.1, s32[2,4,512]{2,1,0:T(4,128)} %owners.1, s32[2,4,512]{2,1,0:T(4,128)} %elements.1, f32[2,2,4,512]{3,2,1,0:T(4,128)} %coords.1, f32[1,512]{1,0:T(1,128)} %bitcast.1, s32[3,512]{1,0:T(4,128)} %neighbours.1, f32[4,512]{1,0:T(4,128)} %lift.1), custom_call_target="tpu_custom_call" | custom-call | tf_op jit(solution)/shard_map/pallas_call | solution.py:333
  17.6 0.7 %copy.9 = f32[4,40,512]{2,1,0:T(8,128)} copy(f32[4,40,512]{2,1,0:T(8,128)S(1)} %shard_map.73) | data formatting | bytes 655360
where the time goes:
time: 18.5 us; the launch traced here: 18.3 us
  Pallas kernels  17.6 us (95%)
  local copies, waits for them, and re-layouts  0.73 us (4%)
    pallas_call x1, Pallas kernels, local(): pl.pallas_call(kernel, out_shape=jax.ShapeDtypeStruct(tracers.shape, F32)...  17.6 us
    unnamed x1, local copies, waits for them, and re-layouts  0.73 us

commit v1 on v0

--- a/solution.py
+++ b/solution.py
@@ -52,7 +52,7 @@
     tracers, owners, elements, coords, mass, neighbours, lift,
     out,
     field_prev, field_own, field_next, own_ids, elem_ids, refs, masses, copies, lifts, prepared,
-    weights1, weights2, shared, inverse, stage0, stage1, stage2, stage3, result, above,
+    units, shared, inverse, result, above,
     local_sem, send_dep, recv_dep, send_field, recv_field, send_up, recv_up,
 ):
     me = lax.axis_index("sfc")
@@ -155,9 +155,8 @@
             prepared[slot, step, level, 1:2, lanes] = refs[slot, step, 0, level : level + 1, lanes]
             prepared[slot, step, level, 2:3, lanes] = refs[slot, step, 1, level : level + 1, lanes]
 
-    def build_weights(slot, row, step, level, target, pair, place):
+    def build_unit(slot, row, step, level, unit):
         lanes = pl.ds(row * ROW, ROW)
-        code = spread(prepared[slot, step, level, 0:1, lanes]).astype(BF16)
         a = spread(prepared[slot, step, level, 1:2, lanes])
         b = spread(prepared[slot, step, level, 2:3, lanes])
         weight = spread(masses[slot, :, lanes]) * scale
@@ -166,19 +165,11 @@
         for point in points_b:
             weight = weight * (b - point)
         high = weight.astype(BF16)
-        low = (weight - high.astype(F32)).astype(BF16)
-        start = ROW * place
-        for number in range(24):
-            hit = code == jnp.asarray(number, BF16)
-            rows = pl.ds(start + 16 * number, 16)
-            target[level, pair, rows, pl.ds(start, ROW)] = jnp.where(hit, high, zero)
-            target[level, pair, rows, pl.ds(256 + start, ROW)] = jnp.where(hit, low, zero)
-        blank = jnp.zeros((ROW, ROW), BF16)
-        rows = pl.ds(0 if place else 384, ROW)
-        target[level, pair, rows, pl.ds(start, ROW)] = blank
-        target[level, pair, rows, pl.ds(256 + start, ROW)] = blank
-
-    def build_shared(slot, row, pair, place):
+        units[level, unit, 0] = spread(prepared[slot, step, level, 0:1, lanes]).astype(BF16)
+        units[level, unit, 1] = high
+        units[level, unit, 2] = (weight - high.astype(F32)).astype(BF16)
+
+    def build_shared(slot, row, place):
         lanes = pl.ds(row * ROW, ROW)
         first = ((me + (slot - 1)) * 4 + (row - 1)) * ROW
         codes, picks = [], []
@@ -188,26 +179,24 @@
             code = jnp.where(copy >= 0, offset >> 4, -1)
             codes.append(spread(code.astype(F32)).astype(BF16))
             picks.append(jnp.where(spread(offset & 15) == node, 1.0, 0.0).astype(BF16))
-        start = ROW * place
         for number in range(24):
             count = jnp.asarray(number, BF16)
-            value = zero
+            value = None
             for code, pick in zip(codes, picks):
-                value = value + jnp.where(code == count, pick, zero)
+                term = jnp.where(code == count, pick, zero)
+                value = term if value is None else value + term
             if 8 <= number < 16:
                 value = value + jnp.where(own_elem == count, own_pick, zero)
-            shared[pair, pl.ds(start + 16 * number, 16), pl.ds(start, ROW)] = value
-        rows = pl.ds(0 if place else 384, ROW)
-        shared[pair, rows, pl.ds(start, ROW)] = jnp.zeros((ROW, ROW), BF16)
+            shared[place, pl.ds(16 * number, 16), :] = value
 
     def moved1_row(extended, level):
-        build_weights(extended // 4, extended % 4, 0, level, weights1, (extended - 1) // 2, (extended - 1) % 2)
+        build_unit(extended // 4, extended % 4, 0, level, extended - 1)
 
     def moved2_row(extended, level):
-        build_weights(extended // 4, extended % 4, 1, level, weights2, (extended - 3) // 2, (extended - 3) % 2)
+        build_unit(extended // 4, extended % 4, 1, level, 7 + extended)
 
     def shared_row(extended):
-        build_shared(extended // 4, extended % 4, (extended - 2) // 2, (extended - 2) % 2)
+        build_shared(extended // 4, extended % 4, extended - 2)
 
     for copy in local:
         copy.wait()
@@ -245,18 +234,34 @@
         mixed = jnp.where(piece == 0, high, jnp.where(piece == 1, middle, jnp.where(piece == 2, low, 0.0)))
         parts.append(mixed.astype(BF16))
     mass_rows = jnp.concatenate(parts, axis=1)
+    blank = jnp.zeros((ROW, ROW), BF16)
+
+    def shared_pair(pair):
+        first = jnp.concatenate([shared[2 * pair], blank], axis=0)
+        second = jnp.concatenate([blank, shared[2 * pair + 1]], axis=0)
+        return jnp.concatenate([first, second], axis=1)
+
     for pair in range(4):
         begin = ROW + 256 * pair
-        total = jnp.dot(mass_rows[:, begin : begin + 512], shared[pair], preferred_element_type=F32)
+        total = jnp.dot(mass_rows[:, begin : begin + 512], shared_pair(pair), preferred_element_type=F32)
         inverse[pair] = 1.0 / jnp.sum(total, axis=0, keepdims=True)
 
-    def interpolate(values, table):
-        product = jnp.dot(values, table, preferred_element_type=F32)
-        low = product[:TRACERS, 256:] + product[TRACERS:, :256] + product[TRACERS:, 256:]
-        return product[:TRACERS, :256] + low
-
-    def average(values, pair):
-        product = jnp.dot(values, shared[pair], preferred_element_type=F32)
+    def interpolate(rows, level, unit):
+        code, high, low = (units[level, unit, part] for part in range(3))
+        hits = [code == jnp.asarray(number, BF16) for number in range(24)]
+        table = jnp.concatenate(
+            [
+                jnp.concatenate([jnp.where(hit, part, zero) for hit in hits], axis=0)
+                for part in (high, low)
+            ],
+            axis=1,
+        )
+        product = jnp.dot(jnp.concatenate(rows, axis=1), table, preferred_element_type=F32)
+        low = product[:TRACERS, ROW:] + product[TRACERS:, :ROW] + product[TRACERS:, ROW:]
+        return split(product[:TRACERS, :ROW] + low)
+
+    def average(rows, pair):
+        product = jnp.dot(jnp.concatenate(rows, axis=1), shared_pair(pair), preferred_element_type=F32)
         return (product[:TRACERS] + product[TRACERS:]) * inverse[pair]
 
     def up_copy():
@@ -274,23 +279,23 @@
             moved1_row(extended, level)
         for extended in (3, 8):
             moved2_row(extended, level)
-        stage0[:, 512:1024] = split(field_own[level])
         for side in range(2):
             field_copy(side, level).wait_recv()
-        stage0[:, :512] = split(field_prev[level])
-        stage0[:, 1024:] = split(field_next[level])
-        for pair in range(5):
-            at = 256 * pair
-            stage1[:, at : at + 256] = split(interpolate(stage0[:, at : at + 512], weights1[level, pair]))
+        rows = {}
+        for slot, block in enumerate((field_prev, field_own, field_next)):
+            for row in range(4):
+                rows[4 * slot + row] = split(block[level, :, ROW * row : ROW * (row + 1)])
+        moved = {e: interpolate([rows[e + k] for k in (-1, 0, 1)], level, e - 1) for e in range(1, 11)}
+        rows = {}
         for pair in range(4):
-            at = 256 * pair
-            stage2[:, at : at + 256] = split(average(stage1[:, at : at + 512], pair))
-        for pair in range(3):
-            at = 256 * pair
-            stage3[:, at : at + 256] = split(interpolate(stage2[:, at : at + 512], weights2[level, pair]))
-        for pair in range(2):
-            at = 256 * pair
-            result[level, :, at : at + 256] = average(stage3[:, at : at + 512], pair + 1)
+            e = 2 + 2 * pair
+            both = split(average([moved[e + k] for k in (-1, 0, 1, 2)], pair))
+            rows[e], rows[e + 1] = both[:, :ROW], both[:, ROW:]
+        moved = {e: interpolate([rows[e + k] for k in (-1, 0, 1)], level, e + 7) for e in range(3, 9)}
+        for pair in (1, 2):
+            e = 2 + 2 * pair
+            at = 256 * (pair - 1)
+            result[level, :, at : at + 256] = average([moved[e + k] for k in (-1, 0, 1, 2)], pair)
 
         @pl.when((level == 0) & (group > 0))
         def _():
@@ -346,14 +351,9 @@
             pltpu.VMEM((3, 3, BLOCK), jnp.int32),
             pltpu.VMEM((LEVELS, BLOCK), F32),
             pltpu.VMEM((3, 2, LEVELS, 3, BLOCK), F32),
-            pltpu.VMEM((LEVELS, 5, 512, 512), BF16),
-            pltpu.VMEM((LEVELS, 3, 512, 512), BF16),
-            pltpu.VMEM((4, 512, 256), BF16),
+            pltpu.VMEM((LEVELS, 16, 3, 16, ROW), BF16),
+            pltpu.VMEM((8, 384, ROW), BF16),
             pltpu.VMEM((4, 1, 256), F32),
-            pltpu.VMEM((2 * TRACERS, 1536), BF16),
-            pltpu.VMEM((2 * TRACERS, 1280), BF16),
-            pltpu.VMEM((2 * TRACERS, 1024), BF16),
-            pltpu.VMEM((2 * TRACERS, 768), BF16),
             pltpu.VMEM((LEVELS, TRACERS, BLOCK), F32),
             pltpu.VMEM((TRACERS, BLOCK), F32),
             dma((7,)),

time: 18.5 us -> 17.7 us (0.957)
  Pallas kernels: 17.6 us -> 16.8 us
    pallas_call x1, Pallas kernels: 17.6 us -> 16.8 us  [local(): pl.pallas_call(kernel, out_shape=jax.ShapeDtypeStruct(tracers.shape, F32)...]
where the time goes in v1:
time: 17.7 us; the launch traced here: 17.6 us
  Pallas kernels  16.8 us (95%)
  local copies, waits for them, and re-layouts  0.73 us (4%)
    pallas_call x1, Pallas kernels, local(): pl.pallas_call(kernel, out_shape=jax.ShapeDtypeStruct(tracers.shape, F32)...  16.8 us
    unnamed x1, local copies, waits for them, and re-layouts  0.73 us

profile of v1, /device:TPU:2, one launch (start us, length us, event | category | flops | bytes accessed | tf_op | source)
XLA Modules:
  0.0 17.6 jit_solution(4672237808558753638)
XLA Ops:
  0.0 16.8 %shard_map.73 = f32[4,40,512]{2,1,0:T(8,128)S(1)} custom-call(f32[4,40,512]{2,1,0:T(8,128)} %tracers.1, s32[2,4,512]{2,1,0:T(4,128)} %owners.1, s32[2,4,512]{2,1,0:T(4,128)} %elements.1, f32[2,2,4,512]{3,2,1,0:T(4,128)} %coords.1, f32[1,512]{1,0:T(1,128)} %bitcast.1, s32[3,512]{1,0:T(4,128)} %neighbours.1, f32[4,512]{1,0:T(4,128)} %lift.1), custom_call_target="tpu_custom_call" | custom-call | tf_op jit(solution)/shard_map/pallas_call | solution.py:338
  16.8 0.7 %copy.9 = f32[4,40,512]{2,1,0:T(8,128)} copy(f32[4,40,512]{2,1,0:T(8,128)S(1)} %shard_map.73) | data formatting | bytes 655360

commit v2 on v1

v2 whole, which is shorter than its diff:
```python
import functools

import jax
import jax.numpy as jnp
from jax import lax
from jax.experimental import pallas as pl
from jax.experimental.pallas import tpu as pltpu
from jax.sharding import PartitionSpec as P

GLL_POINTS = (-1.0, -0.4472135954999579, 0.4472135954999579, 1.0)
MESH = pl.DeviceIdType.MESH
BF16 = jnp.bfloat16
F32 = jnp.float32
LEVELS = 4
TRACERS = 40
ROW = 128
BLOCK = 512


def basis_tables():
    node = lax.broadcasted_iota(jnp.int32, (16, ROW), 0)

    def pick(index, values):
        out = jnp.full((16, ROW), values[3], F32)
        for k in range(3):
            out = jnp.where(index == k, values[k], out)
        return out

    others = [[x for k, x in enumerate(GLL_POINTS) if k != i] for i in range(4)]
    scale = []
    for i in range(4):
        product = 1.0
        for x in others[i]:
            product *= GLL_POINTS[i] - x
        scale.append(1.0 / product)
    first, second = node >> 2, node & 3
    points_a = [pick(first, [others[i][k] for i in range(4)]) for k in range(3)]
    points_b = [pick(second, [others[i][k] for i in range(4)]) for k in range(3)]
    return points_a, points_b, pick(first, scale) * pick(second, scale)


def split(values):
    high = values.astype(BF16).astype(F32)
    return jnp.concatenate([high, values - high], axis=0).astype(BF16)


def spread(row):
    return jnp.broadcast_to(row, (16, ROW))


def kernel(
    tracers, owners, elements, coords, mass, neighbours, lift,
    out,
    fields, own_ids, elem_ids, refs, masses, copies, lifts, prepared,
    units, shared, inverse, rows0, moved1, rows1, moved2, result, above,
    local_sem, send_dep, recv_dep, send_field, recv_field, send_up, recv_up,
):
    me = lax.axis_index("sfc")
    peers = lax.axis_size("sfc")
    group = lax.axis_index("lev")
    groups = lax.axis_size("lev")
    after = lax.rem(me + 1, peers)
    before = lax.rem(me + peers - 1, peers)

    barrier = pltpu.get_barrier_semaphore()
    for device in (before, after):
        pl.semaphore_signal(barrier, inc=1, device_id={"sfc": device}, device_id_type=MESH)

    @pl.when(group < groups - 1)
    def _():
        pl.semaphore_signal(barrier, inc=1, device_id={"lev": group + 1}, device_id_type=MESH)

    local = []

    def fetch(source, target):
        copy = pltpu.make_async_copy(source, target, local_sem.at[len(local)])
        copy.start()
        local.append(copy)

    fetch(owners, own_ids.at[1])
    fetch(elements, elem_ids.at[1])
    fetch(coords, refs.at[1])
    fetch(mass, masses.at[1])
    fetch(neighbours, copies.at[1])
    fetch(lift, lifts)
    fetch(tracers, fields.at[1])

    pl.semaphore_wait(barrier, jnp.where(group > 0, 3, 2))

    odd = lax.rem(me, 2)
    far, near = 0, 1
    device = (jnp.where(odd == 1, after, before), jnp.where(odd == 1, before, after))
    slot_here = (2 * odd, 2 - 2 * odd)
    slot_there = (2 - 2 * odd, 2 * odd)

    def dep_copies(side, slot):
        three = pl.ds(pl.multiple_of((2 - slot) * 64, ROW), BLOCK - ROW)
        one = pl.ds(pl.multiple_of((2 - slot) * 192, ROW), ROW)
        pieces = (
            (owners.at[0, :, three], own_ids.at[slot, 0, :, three]),
            (elements.at[0, :, three], elem_ids.at[slot, 0, :, three]),
            (coords.at[0, :, :, three], refs.at[slot, 0, :, :, three]),
            (mass, masses.at[slot]),
            (neighbours, copies.at[slot]),
            (owners.at[1, :, one], own_ids.at[slot, 1, :, one]),
            (elements.at[1, :, one], elem_ids.at[slot, 1, :, one]),
            (coords.at[1, :, :, one], refs.at[slot, 1, :, :, one]),
        )
        return [
            pltpu.make_async_remote_copy(
                src_ref=source,
                dst_ref=target,
                send_sem=send_dep.at[side, number],
                recv_sem=recv_dep.at[side, number],
                device_id={"sfc": device[side]},
                device_id_type=MESH,
            )
            for number, (source, target) in enumerate(pieces)
        ]

    def field_copy(side, slot, level):
        return pltpu.make_async_remote_copy(
            src_ref=tracers.at[level],
            dst_ref=fields.at[slot, level],
            send_sem=send_field.at[side, level],
            recv_sem=recv_field.at[side, level],
            device_id={"sfc": device[side]},
            device_id_type=MESH,
        )

    for side in (far, near):
        for copy in dep_copies(side, slot_there[side]):
            copy.start()
    for level in range(LEVELS):
        for side in (far, near):
            field_copy(side, slot_there[side], level).start()

    points_a, points_b, scale = basis_tables()
    row_mask = 4 * peers - 1
    point_mask = BLOCK * peers - 1
    node = lax.broadcasted_iota(jnp.int32, (16, ROW), 0)
    lane = lax.broadcasted_iota(jnp.int32, (16, ROW), 1)
    zero = jnp.zeros((16, ROW), BF16)
    own_elem = (8 + (lane >> 4)).astype(F32).astype(BF16)
    own_pick = jnp.where((lane & 15) == node, 1.0, 0.0).astype(BF16)

    def prepare(slot, step, start, count):
        width = count * ROW
        lanes = pl.ds(pl.multiple_of(start * ROW, ROW), width)
        row = lax.broadcasted_iota(jnp.int32, (LEVELS, width), 1) // ROW + start
        elem = elem_ids[slot, step, :, lanes]
        source_row = own_ids[slot, step, :, lanes] * 4 + (elem >> 3)
        above_row = (me + (slot - 1)) * 4 - 1 + row
        offset = (source_row - above_row) & row_mask
        code = (offset * 8 + (elem & 7)).astype(F32)
        first, second = refs[slot, step, 0, :, lanes], refs[slot, step, 1, :, lanes]
        for level in range(LEVELS):
            prepared[slot, step, level, 0:1, lanes] = code[level : level + 1]
            prepared[slot, step, level, 1:2, lanes] = first[level : level + 1]
            prepared[slot, step, level, 2:3, lanes] = second[level : level + 1]

    def build_unit(slot, row, step, level, unit):
        lanes = pl.ds(pl.multiple_of(row * ROW, ROW), ROW)
        a = spread(prepared[slot, step, level, 1:2, lanes])
        b = spread(prepared[slot, step, level, 2:3, lanes])
        weight = spread(masses[slot, :, lanes]) * scale
        for point in points_a:
            weight = weight * (a - point)
        for point in points_b:
            weight = weight * (b - point)
        high = weight.astype(BF16).astype(F32)
        units[level, unit, 0] = spread(prepared[slot, step, level, 0:1, lanes])
        units[level, unit, 1] = high
        units[level, unit, 2] = weight - high

    def build_shared(slot, row, place):
        lanes = pl.ds(pl.multiple_of(row * ROW, ROW), ROW)
        first = ((me + (slot - 1)) * 4 + (row - 1)) * ROW
        codes, picks = [], []
        for number in range(3):
            copy = copies[slot, pl.ds(number, 1), lanes]
            offset = (copy - first) & point_mask
            code = jnp.where(copy >= 0, offset >> 4, -1)
            codes.append(spread(code.astype(F32)).astype(BF16))
            picks.append(jnp.where(spread(offset & 15) == node, 1.0, 0.0).astype(BF16))
        for number in range(24):
            count = jnp.asarray(number, BF16)
            value = None
            for code, pick in zip(codes, picks):
                term = jnp.where(code == count, pick, zero)
                value = term if value is None else value + term
            if 8 <= number < 16:
                value = value + jnp.where(own_elem == count, own_pick, zero)
            shared[place, pl.ds(16 * number, 16), :] = value

    def moved1_unit(slot, row, level):
        build_unit(slot, row, 0, level, 4 * slot + row - 1)

    def moved2_unit(slot, row, level):
        build_unit(slot, row, 1, level, 4 * slot + row + 7)

    for copy in local:
        copy.wait()
    for step in range(2):
        prepare(1, step, 0, 4)

    def own_level(level, carry):
        for row in range(4):
            moved1_unit(1, row, level)
            moved2_unit(1, row, level)
            rows0[level, 4 + row] = split(fields[1, level, :, ROW * row : ROW * (row + 1)])
        return carry

    lax.fori_loop(0, LEVELS, own_level, 0)
    for row in range(4):
        build_shared(1, row, 2 + row)

    blank = jnp.zeros((ROW, ROW), BF16)

    def shared_pair(pair):
        first = jnp.concatenate([shared[2 * pair], blank], axis=0)
        second = jnp.concatenate([blank, shared[2 * pair + 1]], axis=0)
        return jnp.concatenate([first, second], axis=1)

    piece = lax.broadcasted_iota(jnp.int32, (16, ROW), 0)

    def mass_rows(extended):
        lanes = pl.ds(pl.multiple_of((extended % 4) * ROW, ROW), ROW)
        whole = spread(masses[extended // 4, :, lanes])
        high = whole.astype(BF16).astype(F32)
        middle = (whole - high).astype(BF16).astype(F32)
        low = whole - high - middle
        mixed = jnp.where(piece == 0, high, jnp.where(piece == 1, middle, jnp.where(piece == 2, low, 0.0)))
        return mixed.astype(BF16)

    def invert_masses(pair):
        parts = jnp.concatenate([mass_rows(2 * pair + 1 + k) for k in range(4)], axis=1)
        total = jnp.dot(parts, shared_pair(pair), preferred_element_type=F32)
        inverse[pair] = 1.0 / jnp.sum(total, axis=0, keepdims=True)

    def interpolate(source, level, extended, unit):
        code, high, low = (units[level, unit, part].astype(BF16) for part in range(3))
        hits = [code == jnp.asarray(number, BF16) for number in range(24)]
        table = jnp.concatenate(
            [
                jnp.concatenate([jnp.where(hit, part, zero) for hit in hits], axis=0)
                for part in (high, low)
            ],
            axis=1,
        )
        three = source[level, pl.ds(extended - 1, 3)]
        rows = jnp.concatenate([three[k] for k in range(3)], axis=1)
        product = jnp.dot(rows, table, preferred_element_type=F32)
        low = product[:TRACERS, ROW:] + product[TRACERS:, :ROW] + product[TRACERS:, ROW:]
        return product[:TRACERS, :ROW] + low

    def average(source, level, pair):
        four = source[level, pl.ds(2 * pair + 1, 4)]
        rows = jnp.concatenate([four[k] for k in range(4)], axis=1)
        product = jnp.dot(rows, shared_pair(pair), preferred_element_type=F32)
        return (product[:TRACERS] + product[TRACERS:]) * inverse[pair]

    def up_copy():
        return pltpu.make_async_remote_copy(
            src_ref=result.at[0],
            dst_ref=above,
            send_sem=send_up,
            recv_sem=recv_up,
            device_id={"lev": group - 1},
            device_id_type=MESH,
        )

    def first_part(side):
        slot = slot_here[side]
        for copy in dep_copies(side, slot):
            copy.wait_recv()
        inner = 3 - 3 * (slot // 2)
        prepare(slot, 0, 1 - slot // 2, 3)
        prepare(slot, 1, inner, 1)
        pair = 3 * (slot // 2)
        for k in range(2):
            extended = 2 + 2 * pair + k
            build_shared(slot, extended % 4, extended - 2)
        for k in range(2):
            invert_masses(2 * (slot // 2) + k)

    def arrived(side, level):
        slot = slot_here[side]
        for k in range(3):
            moved1_unit(slot, 1 - slot // 2 + k, level)
        moved2_unit(slot, 3 - 3 * (slot // 2), level)
        field_copy(side, slot, level).wait_recv()
        for row in range(4):
            rows0[level, 4 * slot + row] = split(fields[slot, level, :, ROW * row : ROW * (row + 1)])

    def step(level, start1, count1, pairs, start2, count2):
        for k in range(count1):
            moved1[level, start1 + k] = split(interpolate(rows0, level, start1 + k, start1 + k - 1))
        for k in range(2):
            both = split(average(moved1, level, pairs + k))
            rows1[level, 2 + 2 * (pairs + k)] = both[:, :ROW]
            rows1[level, 3 + 2 * (pairs + k)] = both[:, ROW:]
        for k in range(count2):
            moved2[level, start2 + k] = split(interpolate(rows1, level, start2 + k, start2 + k + 7))

    def near_arrivals(half, carry):
        for k in range(2):
            arrived(near, 2 * half + k)
        for k in range(2):
            for row in range(6):
                level, extended = 2 * half + k, 5 - 4 * odd + row
                moved1[level, extended] = split(interpolate(rows0, level, extended, extended - 1))
        return carry

    def near_rest():
        for k in range(2):
            pair = 2 - 2 * odd + k
            levels = [moved1[level, pl.ds(2 * pair + 1, 4)] for level in range(LEVELS)]
            rows = jnp.concatenate([jnp.concatenate([four[j] for j in range(4)], axis=1) for four in levels], axis=0)
            product = jnp.dot(rows, shared_pair(pair), preferred_element_type=F32)
            for level in range(LEVELS):
                high = product[2 * TRACERS * level : 2 * TRACERS * level + TRACERS]
                low = product[2 * TRACERS * level + TRACERS : 2 * TRACERS * (level + 1)]
                both = split((high + low) * inverse[pair])
                rows1[level, 2 + 2 * pair] = both[:, :ROW]
                rows1[level, 3 + 2 * pair] = both[:, ROW:]
        for level in range(LEVELS):
            for k in range(2):
                extended = 7 - 4 * odd + k
                moved2[level, extended] = split(interpolate(rows1, level, extended, extended + 7))

    def far_level(level, carry):
        arrived(far, level)
        step(level, 1 + 6 * odd, 4, 2 * odd, 3 + 2 * odd, 4)
        for pair in (1, 2):
            at = 256 * (pair - 1)
            result[level, :, at : at + 256] = average(moved2, level, pair)

        @pl.when((level == 0) & (group > 0))
        def _():
            up_copy().start()

        return carry

    first_part(near)
    lax.fori_loop(0, LEVELS // 2, near_arrivals, 0)
    near_rest()
    first_part(far)
    lax.fori_loop(0, LEVELS, far_level, 0)

    for level in range(LEVELS - 1):
        field = result[level]
        out[level] = field + lifts[pl.ds(level, 1), :] * (result[level + 1] - field)

    for side in (far, near):
        for copy in dep_copies(side, slot_there[side]):
            copy.wait_send()
        for level in range(LEVELS):
            field_copy(side, slot_there[side], level).wait_send()

    last = LEVELS - 1

    @pl.when(group > 0)
    def _():
        up_copy().wait_send()

    @pl.when(group < groups - 1)
    def _():
        up_copy().wait_recv()
        field = result[last]
        out[last] = field + lifts[pl.ds(last, 1), :] * (above[...] - field)

    @pl.when(group == groups - 1)
    def _():
        field = result[last]
        out[last] = field + lifts[pl.ds(last, 1), :] * (field - field)


def local(tracers, owners, source_elements, ref_coords, node_mass, neighbours, lift_fraction):
    dma = pltpu.SemaphoreType.DMA
    return pl.pallas_call(
        kernel,
        out_shape=jax.ShapeDtypeStruct(tracers.shape, F32),
        in_specs=[pl.BlockSpec(memory_space=pltpu.HBM)] * 7,
        out_specs=pl.BlockSpec(memory_space=pltpu.VMEM),
        scratch_shapes=[
            pltpu.VMEM((3, LEVELS, TRACERS, BLOCK), F32),
            pltpu.VMEM((3, 2, LEVELS, BLOCK), jnp.int32),
            pltpu.VMEM((3, 2, LEVELS, BLOCK), jnp.int32),
            pltpu.VMEM((3, 2, 2, LEVELS, BLOCK), F32),
            pltpu.VMEM((3, 1, BLOCK), F32),
            pltpu.VMEM((3, 3, BLOCK), jnp.int32),
            pltpu.VMEM((LEVELS, BLOCK), F32),
            pltpu.VMEM((3, 2, LEVELS, 3, BLOCK), F32),
            pltpu.VMEM((LEVELS, 16, 3, 16, ROW), F32),
            pltpu.VMEM((8, 384, ROW), BF16),
            pltpu.VMEM((4, 1, 256), F32),
            pltpu.VMEM((LEVELS, 12, 2 * TRACERS, ROW), BF16),
            pltpu.VMEM((LEVELS, 12, 2 * TRACERS, ROW), BF16),
            pltpu.VMEM((LEVELS, 12, 2 * TRACERS, ROW), BF16),
            pltpu.VMEM((LEVELS, 12, 2 * TRACERS, ROW), BF16),
            pltpu.VMEM((LEVELS, TRACERS, BLOCK), F32),
            pltpu.VMEM((TRACERS, BLOCK), F32),
            dma((7,)),
            dma((2, 8)),
            dma((2, 8)),
            dma((2, LEVELS)),
            dma((2, LEVELS)),
            dma,
            dma,
        ],
        compiler_params=pltpu.CompilerParams(
            collective_id=0, has_side_effects=True, vmem_limit_bytes=32 << 20
        ),
    )(*(pltpu.with_memory_space_constraint(x, pltpu.HBM) for x in (tracers, owners, source_elements, ref_coords, node_mass.reshape(1, -1), neighbours, lift_fraction)))


def solution(mesh):
    in_specs = (
        P("lev", None, "sfc"),
        P(None, "lev", "sfc"),
        P(None, "lev", "sfc"),
        P(None, None, "lev", "sfc"),
        P("sfc"),
        P(None, "sfc"),
        P("lev", "sfc"),
    )
    out_specs = P("lev", None, "sfc")
    return jax.shard_map(local, mesh=mesh, in_specs=in_specs, out_specs=out_specs, check_vma=False)
```

time: 17.7 us -> 19.4 us (1.096)
  the two profiles are of different devices: /device:TPU:2 before, /device:TPU:1 now
where the time goes in v2:
time: 19.4 us; the launch traced here: 19.2 us
  Pallas kernels  18.5 us (95%)
  local copies, waits for them, and re-layouts  0.73 us (4%)
    pallas_call x1, Pallas kernels, local(): pl.pallas_call(kernel, out_shape=jax.ShapeDtypeStruct(tracers.shape, F32)...  18.5 us
    unnamed x1, local copies, waits for them, and re-layouts  0.73 us

profile of v2, /device:TPU:1, one launch (start us, length us, event | category | flops | bytes accessed | tf_op | source)
XLA Modules:
  0.0 19.2 jit_solution(13321407397215477081)
XLA Ops:
  0.0 18.5 %shard_map.73 = f32[4,40,512]{2,1,0:T(8,128)S(1)} custom-call(f32[4,40,512]{2,1,0:T(8,128)} %tracers.1, s32[2,4,512]{2,1,0:T(4,128)} %owners.1, s32[2,4,512]{2,1,0:T(4,128)} %elements.1, f32[2,2,4,512]{3,2,1,0:T(4,128)} %coords.1, f32[1,512]{1,0:T(1,128)} %bitcast.1, s32[3,512]{1,0:T(4,128)} %neighbours.1, f32[4,512]{1,0:T(4,128)} %lift.1), custom_call_target="tpu_custom_call" | custom-call | tf_op jit(solution)/shard_map/pallas_call | solution.py:381
  18.5 0.7 %copy.9 = f32[4,40,512]{2,1,0:T(8,128)} copy(f32[4,40,512]{2,1,0:T(8,128)S(1)} %shard_map.73) | data formatting | bytes 655360

commit v3 on v2

--- a/solution.py
+++ b/solution.py
@@ -62,9 +62,20 @@
     after = lax.rem(me + 1, peers)
     before = lax.rem(me + peers - 1, peers)
 
+    odd = lax.rem(me, 2)
+    far, near = 0, 1
+    device = (jnp.where(odd == 1, after, before), jnp.where(odd == 1, before, after))
+    slot_here = (2 * odd, 2 - 2 * odd)
+    slot_there = (2 - 2 * odd, 2 * odd)
+
+    first, last = me == 0, me == peers - 1
+
     barrier = pltpu.get_barrier_semaphore()
-    for device in (before, after):
-        pl.semaphore_signal(barrier, inc=1, device_id={"sfc": device}, device_id_type=MESH)
+    pl.semaphore_signal(barrier, inc=1, device_id={"sfc": device[near]}, device_id_type=MESH)
+
+    @pl.when(jnp.logical_not(last))
+    def _():
+        pl.semaphore_signal(barrier, inc=1, device_id={"sfc": device[far]}, device_id_type=MESH)
 
     @pl.when(group < groups - 1)
     def _():
@@ -85,13 +96,7 @@
     fetch(lift, lifts)
     fetch(tracers, fields.at[1])
 
-    pl.semaphore_wait(barrier, jnp.where(group > 0, 3, 2))
-
-    odd = lax.rem(me, 2)
-    far, near = 0, 1
-    device = (jnp.where(odd == 1, after, before), jnp.where(odd == 1, before, after))
-    slot_here = (2 * odd, 2 - 2 * odd)
-    slot_there = (2 - 2 * odd, 2 * odd)
+    pl.semaphore_wait(barrier, 1 + jnp.where(first, 0, 1) + jnp.where(group > 0, 1, 0))
 
     def dep_copies(side, slot):
         three = pl.ds(pl.multiple_of((2 - slot) * 64, ROW), BLOCK - ROW)
@@ -128,12 +133,17 @@
             device_id_type=MESH,
         )
 
-    for side in (far, near):
+    def send(side):
         for copy in dep_copies(side, slot_there[side]):
             copy.start()
-    for level in range(LEVELS):
-        for side in (far, near):
+        for level in range(LEVELS):
             field_copy(side, slot_there[side], level).start()
+
+    @pl.when(jnp.logical_not(first))
+    def _():
+        send(far)
+
+    send(near)
 
     points_a, points_b, scale = basis_tables()
     row_mask = 4 * peers - 1
@@ -274,6 +284,12 @@
         slot = slot_here[side]
         for copy in dep_copies(side, slot):
             copy.wait_recv()
+        if side == far:
+
+            @pl.when(first)
+            def _():
+                send(far)
+
         inner = 3 - 3 * (slot // 2)
         prepare(slot, 0, 1 - slot // 2, 3)
         prepare(slot, 1, inner, 1)
@@ -358,7 +374,7 @@
         for level in range(LEVELS):
             field_copy(side, slot_there[side], level).wait_send()
 
-    last = LEVELS - 1
+    end = LEVELS - 1
 
     @pl.when(group > 0)
     def _():
@@ -367,13 +383,13 @@
     @pl.when(group < groups - 1)
     def _():
         up_copy().wait_recv()
-        field = result[last]
-        out[last] = field + lifts[pl.ds(last, 1), :] * (above[...] - field)
+        field = result[end]
+        out[end] = field + lifts[pl.ds(end, 1), :] * (above[...] - field)
 
     @pl.when(group == groups - 1)
     def _():
-        field = result[last]
-        out[last] = field + lifts[pl.ds(last, 1), :] * (field - field)
+        field = result[end]
+        out[end] = field + lifts[pl.ds(end, 1), :] * (field - field)
 
 
 def local(tracers, owners, source_elements, ref_coords, node_mass, neighbours, lift_fraction):

time: 19.4 us -> 17.4 us (0.90)
  the two profiles are of different devices: /device:TPU:1 before, /device:TPU:2 now
where the time goes in v3:
time: 17.4 us; the launch traced here: 17.3 us
  Pallas kernels  16.5 us (95%)
  local copies, waits for them, and re-layouts  0.73 us (4%)
    pallas_call x1, Pallas kernels, local(): pl.pallas_call(kernel, out_shape=jax.ShapeDtypeStruct(tracers.shape, F32)...  16.5 us
    unnamed x1, local copies, waits for them, and re-layouts  0.73 us

profile of v3, /device:TPU:2, one launch (start us, length us, event | category | flops | bytes accessed | tf_op | source)
XLA Modules:
  0.0 17.3 jit_solution(520356949484147949)
XLA Ops:
  0.0 16.5 %shard_map.73 = f32[4,40,512]{2,1,0:T(8,128)S(1)} custom-call(f32[4,40,512]{2,1,0:T(8,128)} %tracers.1, s32[2,4,512]{2,1,0:T(4,128)} %owners.1, s32[2,4,512]{2,1,0:T(4,128)} %elements.1, f32[2,2,4,512]{3,2,1,0:T(4,128)} %coords.1, f32[1,512]{1,0:T(1,128)} %bitcast.1, s32[3,512]{1,0:T(4,128)} %neighbours.1, f32[4,512]{1,0:T(4,128)} %lift.1), custom_call_target="tpu_custom_call" | custom-call | tf_op jit(solution)/shard_map/pallas_call | solution.py:397
  16.6 0.7 %copy.9 = f32[4,40,512]{2,1,0:T(8,128)} copy(f32[4,40,512]{2,1,0:T(8,128)S(1)} %shard_map.73) | data formatting | bytes 655360

commit v4 on v3

v4 whole, which is shorter than its diff:
```python
import functools

import jax
import jax.numpy as jnp
from jax import lax
from jax.experimental import pallas as pl
from jax.experimental.pallas import tpu as pltpu
from jax.sharding import PartitionSpec as P

GLL_POINTS = (-1.0, -0.4472135954999579, 0.4472135954999579, 1.0)
MESH = pl.DeviceIdType.MESH
BF16 = jnp.bfloat16
F32 = jnp.float32
LEVELS = 4
TRACERS = 40
ROW = 128
BLOCK = 512


def basis_tables():
    node = lax.broadcasted_iota(jnp.int32, (16, ROW), 0)

    def pick(index, values):
        out = jnp.full((16, ROW), values[3], F32)
        for k in range(3):
            out = jnp.where(index == k, values[k], out)
        return out

    others = [[x for k, x in enumerate(GLL_POINTS) if k != i] for i in range(4)]
    scale = []
    for i in range(4):
        product = 1.0
        for x in others[i]:
            product *= GLL_POINTS[i] - x
        scale.append(1.0 / product)
    first, second = node >> 2, node & 3
    points_a = [pick(first, [others[i][k] for i in range(4)]) for k in range(3)]
    points_b = [pick(second, [others[i][k] for i in range(4)]) for k in range(3)]
    return points_a, points_b, pick(first, scale) * pick(second, scale)


def split(values):
    high = values.astype(BF16).astype(F32)
    return jnp.concatenate([high, values - high], axis=0).astype(BF16)


def spread(row):
    return jnp.broadcast_to(row, (16, ROW))


def kernel(
    tracers, owners, elements, coords, mass, neighbours, lift,
    out,
    fields, own_ids, elem_ids, refs, masses, copies, lifts, prepared, packed, message,
    units, shared, inverse, moved1, rows1, moved2, result, above,
    local_sem, send_dep, recv_dep, send_field, recv_field, send_up, recv_up, token,
):
    me = lax.axis_index("sfc")
    peers = lax.axis_size("sfc")
    group = lax.axis_index("lev")
    groups = lax.axis_size("lev")
    after = lax.rem(me + 1, peers)
    before = lax.rem(me + peers - 1, peers)

    odd = lax.rem(me, 2)
    far, near = 0, 1
    device = (jnp.where(odd == 1, after, before), jnp.where(odd == 1, before, after))
    slot_here = (2 * odd, 2 - 2 * odd)
    slot_there = (2 - 2 * odd, 2 * odd)

    first, last = me == 0, me == peers - 1

    barrier = pltpu.get_barrier_semaphore()
    pl.semaphore_signal(barrier, inc=1, device_id={"sfc": device[near]}, device_id_type=MESH)

    @pl.when(jnp.logical_not(last))
    def _():
        pl.semaphore_signal(barrier, inc=1, device_id={"sfc": device[far]}, device_id_type=MESH)

    @pl.when(group < groups - 1)
    def _():
        pl.semaphore_signal(barrier, inc=1, device_id={"lev": group + 1}, device_id_type=MESH)

    local = []

    def fetch(source, target):
        copy = pltpu.make_async_copy(source, target, local_sem.at[len(local)])
        copy.start()
        local.append(copy)

    fetch(owners, own_ids)
    fetch(elements, elem_ids)
    fetch(coords, refs)
    fetch(mass, masses)
    fetch(neighbours, copies)

    pl.semaphore_wait(barrier, 1 + jnp.where(first, 0, 1) + jnp.where(group > 0, 1, 0))

    @pl.when(last)
    def _():
        pl.semaphore_signal(token, inc=1, device_id={"sfc": device[far]}, device_id_type=MESH)


    def message_copy(side, slot):
        return pltpu.make_async_remote_copy(
            src_ref=packed.at[side],
            dst_ref=message.at[slot],
            send_sem=send_dep.at[side],
            recv_sem=recv_dep.at[side],
            device_id={"sfc": device[side]},
            device_id_type=MESH,
        )

    def field_copy(side, slot, level):
        return pltpu.make_async_remote_copy(
            src_ref=tracers.at[level],
            dst_ref=fields.at[slot, level],
            send_sem=send_field.at[side, level],
            recv_sem=recv_field.at[side, level],
            device_id={"sfc": device[side]},
            device_id_type=MESH,
        )

    points_a, points_b, scale = basis_tables()
    row_mask = 4 * peers - 1
    point_mask = BLOCK * peers - 1
    node = lax.broadcasted_iota(jnp.int32, (16, ROW), 0)
    lane = lax.broadcasted_iota(jnp.int32, (16, ROW), 1)
    zero = jnp.zeros((16, ROW), BF16)
    own_elem = (8 + (lane >> 4)).astype(F32).astype(BF16)
    own_pick = jnp.where((lane & 15) == node, 1.0, 0.0).astype(BF16)

    def prepare(step):
        row = lax.broadcasted_iota(jnp.int32, (LEVELS, BLOCK), 1) // ROW
        elem = elem_ids[step]
        offset = own_ids[step] * 4 + (elem >> 3) - (me * 4 - 1 + row)
        code = ((offset & row_mask) * 8 + (elem & 7)).astype(F32)
        for level in range(LEVELS):
            prepared[step, level, 0:1] = code[level : level + 1]
            prepared[step, level, 1:2] = refs[step, 0, level : level + 1]
            prepared[step, level, 2:3] = refs[step, 1, level : level + 1]

    def pack(side):
        slot = slot_there[side]
        start = (2 - slot) * 64
        three = pl.ds(pl.multiple_of(start, ROW), 3 * ROW)
        one = pl.ds(pl.multiple_of(3 * start, ROW), ROW)
        two = pl.ds(pl.multiple_of(2 * start, ROW), 2 * ROW)
        for level in range(LEVELS):
            packed[side, level, 0:3, 0:384] = prepared[0, level, 0:3, three]
            packed[side, level, 0:3, 384:512] = prepared[1, level, 0:3, one]
        packed[side, 0, 3:4, 0:384] = masses[:, three]
        packed[side, 0, 3:4, 384:512] = jnp.zeros((1, ROW), F32)
        for number in range(3):
            packed[side, 1 + number, 3:4, 0:256] = copies[number : number + 1, two].astype(F32)
            packed[side, 1 + number, 3:4, 256:512] = jnp.zeros((1, 256), F32)

    for copy in local[:5]:
        copy.wait()
    for step in range(2):
        prepare(step)
    pack(far)

    @pl.when(jnp.logical_not(first))
    def _():
        message_copy(far, slot_there[far]).start()
        for level in range(LEVELS):
            field_copy(far, slot_there[far], level).start()

    fetch(lift, lifts)
    fetch(tracers, fields.at[1])
    pack(near)
    message_copy(near, slot_there[near]).start()
    for level in range(LEVELS):
        field_copy(near, slot_there[near], level).start()

    def build_unit(point, weight_row, level, unit):
        a = spread(point[1:2])
        b = spread(point[2:3])
        weight = spread(weight_row) * scale
        for x in points_a:
            weight = weight * (a - x)
        for x in points_b:
            weight = weight * (b - x)
        high = weight.astype(BF16).astype(F32)
        units[level, unit, 0] = spread(point[0:1])
        units[level, unit, 1] = high
        units[level, unit, 2] = weight - high

    def build_shared(slot, row, links, place):
        first_node = ((me + (slot - 1)) * 4 + (row - 1)) * ROW
        codes, picks = [], []
        for number in range(3):
            copy = links[number]
            offset = (copy - first_node) & point_mask
            code = jnp.where(copy >= 0, offset >> 4, -1)
            codes.append(spread(code.astype(F32)).astype(BF16))
            picks.append(jnp.where(spread(offset & 15) == node, 1.0, 0.0).astype(BF16))
        for number in range(24):
            count = jnp.asarray(number, BF16)
            value = None
            for code, pick in zip(codes, picks):
                term = jnp.where(code == count, pick, zero)
                value = term if value is None else value + term
            if 8 <= number < 16:
                value = value + jnp.where(own_elem == count, own_pick, zero)
            shared[place, pl.ds(16 * number, 16), :] = value

    def lanes_of(row):
        return slice(ROW * row, ROW * (row + 1))

    def own_level(level, carry):
        for row in range(4):
            at = lanes_of(row)
            build_unit(prepared[0, level, 0:3, at], masses[:, at], level, 3 + row)
            build_unit(prepared[1, level, 0:3, at], masses[:, at], level, 11 + row)
        return carry

    lax.fori_loop(0, LEVELS, own_level, 0)
    for row in range(4):
        build_shared(1, row, [copies[k : k + 1, lanes_of(row)] for k in range(3)], 2 + row)
    for copy in local[5:]:
        copy.wait()

    blank = jnp.zeros((ROW, ROW), BF16)

    def shared_pair(pair):
        first = jnp.concatenate([shared[2 * pair], blank], axis=0)
        second = jnp.concatenate([blank, shared[2 * pair + 1]], axis=0)
        return jnp.concatenate([first, second], axis=1)

    piece = lax.broadcasted_iota(jnp.int32, (16, ROW), 0)

    def mass_parts(row):
        whole = spread(row)
        high = whole.astype(BF16).astype(F32)
        middle = (whole - high).astype(BF16).astype(F32)
        low = whole - high - middle
        mixed = jnp.where(piece == 0, high, jnp.where(piece == 1, middle, jnp.where(piece == 2, low, 0.0)))
        return mixed.astype(BF16)

    def invert_masses(rows, pair):
        parts = jnp.concatenate([mass_parts(row) for row in rows], axis=1)
        total = jnp.dot(parts, shared_pair(pair), preferred_element_type=F32)
        inverse[pair] = 1.0 / jnp.sum(total, axis=0, keepdims=True)

    def interpolate(rows, level, unit):
        code, high, low = (units[level, unit, part].astype(BF16) for part in range(3))
        hits = [code == jnp.asarray(number, BF16) for number in range(24)]
        table = jnp.concatenate(
            [
                jnp.concatenate([jnp.where(hit, part, zero) for hit in hits], axis=0)
                for part in (high, low)
            ],
            axis=1,
        )
        product = jnp.dot(jnp.concatenate(rows, axis=1), table, preferred_element_type=F32)
        low = product[:TRACERS, ROW:] + product[TRACERS:, :ROW] + product[TRACERS:, ROW:]
        return product[:TRACERS, :ROW] + low

    def average(rows, pair):
        product = jnp.dot(jnp.concatenate(rows, axis=1), shared_pair(pair), preferred_element_type=F32)
        return (product[:TRACERS] + product[TRACERS:]) * inverse[pair]

    def up_copy():
        return pltpu.make_async_remote_copy(
            src_ref=result.at[0],
            dst_ref=above,
            send_sem=send_up,
            recv_sem=recv_up,
            device_id={"lev": group - 1},
            device_id_type=MESH,
        )

    def first_part(side, slot):
        message_copy(side, slot).wait_recv()
        below = slot == 2
        for k in range(2):
            links = [message[slot, 1 + number, 3:4, lanes_of(k)].astype(jnp.int32) for number in range(3)]
            build_shared(slot, k if below else 2 + k, links, (6 if below else 0) + k)
        theirs = [message[slot, 0, 3:4, lanes_of(k)] for k in range(3)]
        own = [masses[:, lanes_of(row)] for row in range(4)]
        rows = own + theirs if below else theirs + own
        for k in range(2):
            begin = (1 if below else 0) + 2 * k
            invert_masses(rows[begin : begin + 4], (2 if below else 0) + k)

    def arrived(side, slot, level):
        weight_rows = [message[slot, 0, 3:4, lanes_of(k)] for k in range(3)]
        for k in range(3):
            build_unit(message[slot, level, 0:3, lanes_of(k)], weight_rows[k], level, (7 if slot == 2 else 0) + k)
        beside = 0 if slot == 2 else 2
        build_unit(message[slot, level, 0:3, lanes_of(3)], weight_rows[beside], level, 15 if slot == 2 else 10)
        field_copy(side, slot, level).wait_recv()

    def field_row(extended, level):
        row = extended % 4
        return split(fields[extended // 4, level, :, ROW * row : ROW * (row + 1)])

    def around(rows, extended, count):
        return [rows[extended + k - 1] for k in range(count)]

    def near_part(parity):
        slot, begin, first_pair = 2 - 2 * parity, 5 - 4 * parity, 2 - 2 * parity
        first_part(near, slot)

        def arrivals(half, carry):
            levels = [2 * half + k for k in range(2)]
            for level in levels:
                arrived(near, slot, level)
            for level in levels:
                rows = {e: field_row(e, level) for e in range(begin - 1, begin + 7)}
                for e in range(begin, begin + 6):
                    moved1[level, e] = split(interpolate(around(rows, e, 3), level, e - 1))
            return carry

        lax.fori_loop(0, LEVELS // 2, arrivals, 0)
        fields1 = [{} for _ in range(LEVELS)]
        for pair in (first_pair, first_pair + 1):
            e = 2 + 2 * pair
            rows = [jnp.concatenate([moved1[level, e + k - 1] for k in range(4)], axis=1) for level in range(LEVELS)]
            product = jnp.dot(jnp.concatenate(rows, axis=0), shared_pair(pair), preferred_element_type=F32)
            for level in range(LEVELS):
                start = 2 * TRACERS * level
                total = product[start : start + TRACERS] + product[start + TRACERS : start + 2 * TRACERS]
                both = split(total * inverse[pair])
                for k in range(2):
                    fields1[level][e + k] = both[:, ROW * k : ROW * (k + 1)]
                    rows1[level, e + k] = fields1[level][e + k]
        for level in range(LEVELS):
            for e in (begin + 2, begin + 3):
                moved2[level, e] = split(interpolate(around(fields1[level], e, 3), level, e + 7))

    def remap(level):
        field = result[level]
        out[level] = field + lifts[pl.ds(level, 1), :] * (result[level + 1] - field)

    def far_part(parity):
        slot, begin, first_pair, begin2 = 2 * parity, 1 + 6 * parity, 2 * parity, 3 + 2 * parity
        first_part(far, slot)

        def one_level(level, carry):
            arrived(far, slot, level)
            rows = {e: field_row(e, level) for e in range(begin - 1, begin + 5)}
            moved = {e: split(interpolate(around(rows, e, 3), level, e - 1)) for e in range(begin, begin + 4)}
            for e in (5, 6):
                moved[e] = moved1[level, e]
            rows = {e: rows1[level, e] for e in (6 - 2 * parity, 7 - 2 * parity)}
            for pair in (first_pair, first_pair + 1):
                e = 2 + 2 * pair
                both = split(average(around(moved, e, 4), pair))
                rows[e], rows[e + 1] = both[:, :ROW], both[:, ROW:]
            moved = {e: moved2[level, e] for e in (7 - 4 * parity, 8 - 4 * parity)}
            for e in range(begin2, begin2 + 4):
                moved[e] = split(interpolate(around(rows, e, 3), level, e + 7))
            for pair in (1, 2):
                at = 256 * (pair - 1)
                result[level, :, at : at + 256] = average(around(moved, 2 + 2 * pair, 4), pair)

            @pl.when((level == 0) & (group > 0))
            def _():
                up_copy().start()

            return carry

        lax.fori_loop(0, LEVELS, one_level, 0)

    def by_parity(part):
        @pl.when(odd == 0)
        def _():
            part(0)

        @pl.when(odd == 1)
        def _():
            part(1)

    by_parity(near_part)

    @pl.when(first)
    def _():
        pl.semaphore_wait(token, 1)
        message_copy(far, slot_there[far]).start()
        for level in range(LEVELS):
            field_copy(far, slot_there[far], level).start()

    by_parity(far_part)

    for level in range(LEVELS - 1):
        remap(level)

    for side in (far, near):
        message_copy(side, slot_there[side]).wait_send()
        for level in range(LEVELS):
            field_copy(side, slot_there[side], level).wait_send()

    end = LEVELS - 1

    @pl.when(group > 0)
    def _():
        up_copy().wait_send()

    @pl.when(group < groups - 1)
    def _():
        up_copy().wait_recv()
        field = result[end]
        out[end] = field + lifts[pl.ds(end, 1), :] * (above[...] - field)

    @pl.when(group == groups - 1)
    def _():
        field = result[end]
        out[end] = field + lifts[pl.ds(end, 1), :] * (field - field)


def local(tracers, owners, source_elements, ref_coords, node_mass, neighbours, lift_fraction):
    dma = pltpu.SemaphoreType.DMA
    return pl.pallas_call(
        kernel,
        out_shape=jax.ShapeDtypeStruct(tracers.shape, F32),
        in_specs=[pl.BlockSpec(memory_space=pltpu.HBM)] * 7,
        out_specs=pl.BlockSpec(memory_space=pltpu.VMEM),
        scratch_shapes=[
            pltpu.VMEM((3, LEVELS, TRACERS, BLOCK), F32),
            pltpu.VMEM((2, LEVELS, BLOCK), jnp.int32),
            pltpu.VMEM((2, LEVELS, BLOCK), jnp.int32),
            pltpu.VMEM((2, 2, LEVELS, BLOCK), F32),
            pltpu.VMEM((1, BLOCK), F32),
            pltpu.VMEM((3, BLOCK), jnp.int32),
            pltpu.VMEM((LEVELS, BLOCK), F32),
            pltpu.VMEM((2, LEVELS, 3, BLOCK), F32),
            pltpu.VMEM((2, LEVELS, 4, BLOCK), F32),
            pltpu.VMEM((3, LEVELS, 4, BLOCK), F32),
            pltpu.VMEM((LEVELS, 16, 3, 16, ROW), F32),
            pltpu.VMEM((8, 384, ROW), BF16),
            pltpu.VMEM((4, 1, 256), F32),
            pltpu.VMEM((LEVELS, 12, 2 * TRACERS, ROW), BF16),
            pltpu.VMEM((LEVELS, 12, 2 * TRACERS, ROW), BF16),
            pltpu.VMEM((LEVELS, 12, 2 * TRACERS, ROW), BF16),
            pltpu.VMEM((LEVELS, TRACERS, BLOCK), F32),
            pltpu.VMEM((TRACERS, BLOCK), F32),
            dma((7,)),
            dma((2,)),
            dma((2,)),
            dma((2, LEVELS)),
            dma((2, LEVELS)),
            dma,
            dma,
            pltpu.SemaphoreType.REGULAR,
        ],
        compiler_params=pltpu.CompilerParams(
            collective_id=0, has_side_effects=True, vmem_limit_bytes=32 << 20
        ),
    )(*(pltpu.with_memory_space_constraint(x, pltpu.HBM) for x in (tracers, owners, source_elements, ref_coords, node_mass.reshape(1, -1), neighbours, lift_fraction)))


def solution(mesh):
    in_specs = (
        P("lev", None, "sfc"),
        P(None, "lev", "sfc"),
        P(None, "lev", "sfc"),
        P(None, None, "lev", "sfc"),
        P("sfc"),
        P(None, "sfc"),
        P("lev", "sfc"),
    )
    out_specs = P("lev", None, "sfc")
    return jax.shard_map(local, mesh=mesh, in_specs=in_specs, out_specs=out_specs, check_vma=False)
```

time: 17.4 us -> 17.1 us (0.983)
  Pallas kernels: 16.5 us -> 16.1 us
    pallas_call x1, Pallas kernels: 16.5 us -> 16.1 us  [local(): pl.pallas_call(kernel, out_shape=jax.ShapeDtypeStruct(tracers.shape, F32)...]
where the time goes in v4:
time: 17.1 us; the launch traced here: 16.8 us
  Pallas kernels  16.1 us (94%)
  local copies, waits for them, and re-layouts  0.73 us (4%)
    pallas_call x1, Pallas kernels, local(): pl.pallas_call(kernel, out_shape=jax.ShapeDtypeStruct(tracers.shape, F32)...  16.1 us
    unnamed x1, local copies, waits for them, and re-layouts  0.73 us

profile of v4, /device:TPU:2, one launch (start us, length us, event | category | flops | bytes accessed | tf_op | source)
XLA Modules:
  0.0 16.8 jit_solution(14422863926585551553)
XLA Ops:
  0.0 16.1 %shard_map.73 = f32[4,40,512]{2,1,0:T(8,128)S(1)} custom-call(f32[4,40,512]{2,1,0:T(8,128)} %tracers.1, s32[2,4,512]{2,1,0:T(4,128)} %owners.1, s32[2,4,512]{2,1,0:T(4,128)} %elements.1, f32[2,2,4,512]{3,2,1,0:T(4,128)} %coords.1, f32[1,512]{1,0:T(1,128)} %bitcast.1, s32[3,512]{1,0:T(4,128)} %neighbours.1, f32[4,512]{1,0:T(4,128)} %lift.1), custom_call_target="tpu_custom_call" | custom-call | tf_op jit(solution)/shard_map/pallas_call | solution.py:416
  16.1 0.7 %copy.9 = f32[4,40,512]{2,1,0:T(8,128)} copy(f32[4,40,512]{2,1,0:T(8,128)S(1)} %shard_map.73) | data formatting | bytes 655360

commit v5 on v4

--- a/solution.py
+++ b/solution.py
@@ -53,7 +53,7 @@
     out,
     fields, own_ids, elem_ids, refs, masses, copies, lifts, prepared, packed, message,
     units, shared, inverse, moved1, rows1, moved2, result, above,
-    local_sem, send_dep, recv_dep, send_field, recv_field, send_up, recv_up, token,
+    local_sem, send_dep, recv_dep, send_field, recv_field, send_half, recv_half, send_up, recv_up, token,
 ):
     me = lax.axis_index("sfc")
     peers = lax.axis_size("sfc")
@@ -120,6 +120,23 @@
             device_id={"sfc": device[side]},
             device_id_type=MESH,
         )
+
+    def half_copy(slot, part):
+        start = (2 - slot) * ROW if part == 0 else slot * ROW
+        lanes = pl.ds(start if isinstance(start, int) else pl.multiple_of(start, ROW), 2 * ROW)
+        return pltpu.make_async_remote_copy(
+            src_ref=tracers.at[0, :, lanes],
+            dst_ref=fields.at[slot, 0, :, lanes],
+            send_sem=send_half.at[part],
+            recv_sem=recv_half.at[part],
+            device_id={"sfc": device[far]},
+            device_id_type=MESH,
+        )
+
+    def far_copies():
+        slot = slot_there[far]
+        halves = [half_copy(slot, part) for part in range(2)]
+        return [message_copy(far, slot)] + halves + [field_copy(far, slot, level) for level in range(1, LEVELS)]
 
     points_a, points_b, scale = basis_tables()
     row_mask = 4 * peers - 1
@@ -163,9 +180,8 @@
 
     @pl.when(jnp.logical_not(first))
     def _():
-        message_copy(far, slot_there[far]).start()
-        for level in range(LEVELS):
-            field_copy(far, slot_there[far], level).start()
+        for copy in far_copies():
+            copy.start()
 
     fetch(lift, lifts)
     fetch(tracers, fields.at[1])
@@ -262,12 +278,12 @@
         product = jnp.dot(jnp.concatenate(rows, axis=1), shared_pair(pair), preferred_element_type=F32)
         return (product[:TRACERS] + product[TRACERS:]) * inverse[pair]
 
-    def up_copy():
+    def up_copy(half):
         return pltpu.make_async_remote_copy(
-            src_ref=result.at[0],
-            dst_ref=above,
-            send_sem=send_up,
-            recv_sem=recv_up,
+            src_ref=result.at[0, :, pl.ds(256 * half, 256)],
+            dst_ref=above.at[:, pl.ds(256 * half, 256)],
+            send_sem=send_up.at[half],
+            recv_sem=recv_up.at[half],
             device_id={"lev": group - 1},
             device_id_type=MESH,
         )
@@ -285,12 +301,15 @@
             begin = (1 if below else 0) + 2 * k
             invert_masses(rows[begin : begin + 4], (2 if below else 0) + k)
 
-    def arrived(side, slot, level):
+    def their_units(slot, level):
         weight_rows = [message[slot, 0, 3:4, lanes_of(k)] for k in range(3)]
         for k in range(3):
             build_unit(message[slot, level, 0:3, lanes_of(k)], weight_rows[k], level, (7 if slot == 2 else 0) + k)
         beside = 0 if slot == 2 else 2
         build_unit(message[slot, level, 0:3, lanes_of(3)], weight_rows[beside], level, 15 if slot == 2 else 10)
+
+    def arrived(side, slot, level):
+        their_units(slot, level)
         field_copy(side, slot, level).wait_recv()
 
     def field_row(extended, level):
@@ -357,13 +376,36 @@
                 at = 256 * (pair - 1)
                 result[level, :, at : at + 256] = average(around(moved, 2 + 2 * pair, 4), pair)
 
-            @pl.when((level == 0) & (group > 0))
-            def _():
-                up_copy().start()
-
             return carry
 
-        lax.fori_loop(0, LEVELS, one_level, 0)
+        their_units(slot, 0)
+        moved = {e: moved1[0, e] for e in (5, 6)}
+        fields1 = {e: rows1[0, e] for e in (6 - 2 * parity, 7 - 2 * parity)}
+        last_moved = {e: moved2[0, e] for e in (7 - 4 * parity, 8 - 4 * parity)}
+        rows = {e: field_row(e, 0) for e in (4 + 2 * parity, 5 + 2 * parity)}
+        for part in range(2):
+            half_copy(slot, part).wait_recv()
+            near_row = 8 + 2 * part if parity else 2 - 2 * part
+            for e in (near_row, near_row + 1):
+                rows[e] = field_row(e, 0)
+            e = 7 + 2 * part if parity else 3 - 2 * part
+            for e in (e, e + 1):
+                moved[e] = split(interpolate(around(rows, e, 3), 0, e - 1))
+            pair = 2 + part if parity else 1 - part
+            both = split(average(around(moved, 2 + 2 * pair, 4), pair))
+            fields1[2 + 2 * pair], fields1[3 + 2 * pair] = both[:, :ROW], both[:, ROW:]
+            e = 5 + 2 * part if parity else 5 - 2 * part
+            for e in (e, e + 1):
+                last_moved[e] = split(interpolate(around(fields1, e, 3), 0, e + 7))
+            pair = 1 + part if parity else 2 - part
+            at = 256 * (pair - 1)
+            result[0, :, at : at + 256] = average(around(last_moved, 2 + 2 * pair, 4), pair)
+
+            @pl.when(group > 0)
+            def _(half=pair - 1):
+                up_copy(half).start()
+
+        lax.fori_loop(1, LEVELS, one_level, 0)
 
     def by_parity(part):
         @pl.when(odd == 0)
@@ -379,29 +421,31 @@
     @pl.when(first)
     def _():
         pl.semaphore_wait(token, 1)
-        message_copy(far, slot_there[far]).start()
-        for level in range(LEVELS):
-            field_copy(far, slot_there[far], level).start()
+        for copy in far_copies():
+            copy.start()
 
     by_parity(far_part)
 
     for level in range(LEVELS - 1):
         remap(level)
 
-    for side in (far, near):
-        message_copy(side, slot_there[side]).wait_send()
-        for level in range(LEVELS):
-            field_copy(side, slot_there[side], level).wait_send()
+    for copy in far_copies():
+        copy.wait_send()
+    message_copy(near, slot_there[near]).wait_send()
+    for level in range(LEVELS):
+        field_copy(near, slot_there[near], level).wait_send()
 
     end = LEVELS - 1
 
     @pl.when(group > 0)
     def _():
-        up_copy().wait_send()
+        for half in range(2):
+            up_copy(half).wait_send()
 
     @pl.when(group < groups - 1)
     def _():
-        up_copy().wait_recv()
+        for half in range(2):
+            up_copy(half).wait_recv()
         field = result[end]
         out[end] = field + lifts[pl.ds(end, 1), :] * (above[...] - field)
 
@@ -442,8 +486,10 @@
             dma((2,)),
             dma((2, LEVELS)),
             dma((2, LEVELS)),
-            dma,
-            dma,
+            dma((2,)),
+            dma((2,)),
+            dma((2,)),
+            dma((2,)),
             pltpu.SemaphoreType.REGULAR,
         ],
         compiler_params=pltpu.CompilerParams(

time: 17.1 us -> 16.9 us (0.988)
  Pallas kernels: 16.1 us -> 15.9 us
    pallas_call x1, Pallas kernels: 16.1 us -> 15.9 us  [local(): pl.pallas_call(kernel, out_shape=jax.ShapeDtypeStruct(tracers.shape, F32)...]
where the time goes in v5:
time: 16.9 us; the launch traced here: 16.6 us
  Pallas kernels  15.9 us (94%)
  local copies, waits for them, and re-layouts  0.73 us (4%)
    pallas_call x1, Pallas kernels, local(): pl.pallas_call(kernel, out_shape=jax.ShapeDtypeStruct(tracers.shape, F32)...  15.9 us
    unnamed x1, local copies, waits for them, and re-layouts  0.73 us

profile of v5, /device:TPU:2, one launch (start us, length us, event | category | flops | bytes accessed | tf_op | source)
XLA Modules:
  0.0 16.6 jit_solution(13189018629174094418)
XLA Ops:
  0.0 15.9 %shard_map.73 = f32[4,40,512]{2,1,0:T(8,128)S(1)} custom-call(f32[4,40,512]{2,1,0:T(8,128)} %tracers.1, s32[2,4,512]{2,1,0:T(4,128)} %owners.1, s32[2,4,512]{2,1,0:T(4,128)} %elements.1, f32[2,2,4,512]{3,2,1,0:T(4,128)} %coords.1, f32[1,512]{1,0:T(1,128)} %bitcast.1, s32[3,512]{1,0:T(4,128)} %neighbours.1, f32[4,512]{1,0:T(4,128)} %lift.1), custom_call_target="tpu_custom_call" | custom-call | tf_op jit(solution)/shard_map/pallas_call | solution.py:460
  15.9 0.7 %copy.9 = f32[4,40,512]{2,1,0:T(8,128)} copy(f32[4,40,512]{2,1,0:T(8,128)S(1)} %shard_map.73) | data formatting | bytes 655360
